TPU v7x, 32 devices: a whole 2x2x4 slice. The times are simulated.
32 devices in a mesh: dp: 8 (over y, x, core), tensor: 4 (over z).
Axes of the slice: x: 2, y: 2, z: 4, core: 2. Of those that a mesh axis runs over, the one named last changes fastest.
Arguments:
- patches: bfloat16 [16384, 1024], P('dp'), may hold values from -6 to 6
- pos_embed: bfloat16 [16384, 1024], P('dp'), may hold values from -6 to 6
- counts: int32 [8, 8], P('dp'), may hold values from 96 to 576, as said below
- ln1_gain: float32 [1024], replicated, may hold values from 0.5 to 1.5
- w_qkv: bfloat16 [1024, 3, 1024], P(None, None, 'tensor'), may hold values from -0.1875 to 0.1875
- w_out: bfloat16 [1024, 1024], P('tensor'), may hold values from -0.75 to 0.75
- ln2_gain: float32 [1024], replicated, may hold values from 0.5 to 1.5
- w_up: bfloat16 [1024, 4096], P(None, 'tensor'), may hold values from -0.1875 to 0.1875
- w_down: bfloat16 [4096, 1024], P('tensor'), may hold values from -0.09375 to 0.09375
- ln3_gain: float32 [1024], replicated, may hold values from 0.5 to 1.5
- w_learn1: bfloat16 [1024, 1024], replicated, may hold values from -0.1875 to 0.1875
- w_learn2: bfloat16 [1024, 8], replicated, may hold values from -0.1875 to 0.1875
- cotangent: bfloat16 [64, 8, 1024], P('dp'), may hold values from -48 to 48
Outputs:
- learned: bfloat16 [64, 8, 1024], P('dp')
- input_grad: bfloat16 [16384, 1024], P('dp')
- grad_ln1_gain: float32 [1024], replicated
- grad_w_qkv: float32 [1024, 3, 1024], P(None, None, 'tensor')
- grad_w_out: float32 [1024, 1024], P('tensor')
- grad_ln2_gain: float32 [1024], replicated
- grad_w_up: float32 [1024, 4096], P(None, 'tensor')
- grad_w_down: float32 [4096, 1024], P('tensor')
- grad_ln3_gain: float32 [1024], replicated
- grad_w_learn1: float32 [1024, 1024], replicated
- grad_w_learn2: float32 [1024, 8], replicated
Inputs may be any that keep to these rules, and one draw needn't show every extreme that they name: Each row of 8 counts sums to 2048, and the largest of each row is 576.
All inputs are finite; a program needn't handle non-finite values.
Results may differ from a plain program's by a relative error of at most 0.019.
Values may be sent and summed in bfloat16 or wider, within the bound.
No kernel may reach another device: no remote copies, remote signals or barrier semaphores. Data moves between devices by JAX's collectives and lax.ppermute only.
A program may use at most 256 MiB of HBM per device.

v0:
```python
import jax
import jax.numpy as jnp
from jax import lax
from jax.sharding import PartitionSpec as P

HEAD_DIM = 64
MOST = 576
BLOCK = 512
WINDOW = 1664
EPSILON = 1e-06
LOW_TYPE = jnp.bfloat16
WIDE_TYPE = jnp.float32


def layer_norm(values, gain_vector):
    center = values - jnp.mean(values, axis=-1, keepdims=True)
    variance = jnp.mean(center * center, axis=-1, keepdims=True)
    inverse = lax.rsqrt(variance + EPSILON)
    normed = center * inverse
    return (normed * gain_vector, normed, inverse)


def norm_back(grad_in, gain_vector, normed, inverse):
    gain_grad = jnp.sum(grad_in * normed, axis=0)
    scaled = grad_in * gain_vector
    result = (
        scaled
        - jnp.mean(scaled, axis=-1, keepdims=True)
        - normed * jnp.mean(scaled * normed, axis=-1, keepdims=True)
    ) * inverse
    return (result, gain_grad)


def gelu_exact(values):
    return jax.nn.gelu(values, approximate=False)


def gelu_grad(values, upstream):
    pullback = jax.vjp(gelu_exact, values)[1]
    return pullback(upstream)[0]


def image_ids(counts_row, row_count):
    ends = jnp.cumsum(counts_row)
    places = jnp.arange(row_count, dtype=jnp.int32)
    return jnp.sum((places[:, None] >= ends[None, :]).astype(jnp.int32), axis=1)


def block_pieces(query, keys, values, image_of, block_index, score_scale):
    row_count = query.shape[0]
    query_start = block_index * BLOCK
    key_start = jnp.clip(query_start - MOST, 0, row_count - WINDOW)
    query_block = lax.dynamic_slice_in_dim(query, query_start, BLOCK, 0)
    key_block = lax.dynamic_slice_in_dim(keys, key_start, WINDOW, 0)
    value_block = lax.dynamic_slice_in_dim(values, key_start, WINDOW, 0)
    query_ids = lax.dynamic_slice_in_dim(image_of, query_start, BLOCK, 0)
    key_ids = lax.dynamic_slice_in_dim(image_of, key_start, WINDOW, 0)
    scores = (
        jnp.einsum("qhd,khd->hqk", query_block, key_block, preferred_element_type=WIDE_TYPE)
        * score_scale
    )
    allowed = (query_ids[:, None] == key_ids[None, :])[None]
    scores = jnp.where(allowed, scores, -1e30)
    return (query_start, key_start, query_block, key_block, value_block, scores)


def attend_forward(query, keys, values, image_of, score_scale):
    row_count = query.shape[0]

    def one_block(block_index):
        pieces = block_pieces(query, keys, values, image_of, block_index, score_scale)
        value_block = pieces[4]
        scores = pieces[5]
        row_max = jnp.max(scores, axis=-1, keepdims=True)
        exponent = jnp.exp(scores - row_max)
        row_total = jnp.sum(exponent, axis=-1, keepdims=True)
        probs = (exponent / row_total).astype(LOW_TYPE)
        result = jnp.einsum("hqk,khd->qhd", probs, value_block, preferred_element_type=WIDE_TYPE)
        return (result.astype(LOW_TYPE), row_max + jnp.log(row_total))

    outputs, log_sums = lax.map(one_block, jnp.arange(row_count // BLOCK, dtype=jnp.int32))
    return (outputs.reshape(query.shape), log_sums)


def attend_backward(query, keys, values, image_of, log_sums, grad_mixed, score_scale):
    row_count = query.shape[0]

    def one_block(block_index, carried):
        grad_query, grad_keys, grad_values = carried
        pieces = block_pieces(query, keys, values, image_of, block_index, score_scale)
        query_start, key_start, query_block, key_block, value_block, scores = pieces
        grad_block = lax.dynamic_slice_in_dim(grad_mixed, query_start, BLOCK, 0)
        probs = jnp.exp(scores - log_sums[block_index])
        grad_probs = jnp.einsum(
            "qhd,khd->hqk", grad_block, value_block, preferred_element_type=WIDE_TYPE
        )
        inner_sum = jnp.sum(probs * grad_probs, axis=-1, keepdims=True)
        grad_scores = (probs * (grad_probs - inner_sum)).astype(LOW_TYPE)
        query_part = (
            jnp.einsum("hqk,khd->qhd", grad_scores, key_block, preferred_element_type=WIDE_TYPE)
            * score_scale
        )
        key_part = (
            jnp.einsum("hqk,qhd->khd", grad_scores, query_block, preferred_element_type=WIDE_TYPE)
            * score_scale
        )
        value_part = jnp.einsum(
            "hqk,qhd->khd", probs.astype(LOW_TYPE), grad_block, preferred_element_type=WIDE_TYPE
        )
        grad_query = lax.dynamic_update_slice_in_dim(grad_query, query_part, query_start, 0)
        key_window = lax.dynamic_slice_in_dim(grad_keys, key_start, WINDOW, 0) + key_part
        grad_keys = lax.dynamic_update_slice_in_dim(grad_keys, key_window, key_start, 0)
        value_window = lax.dynamic_slice_in_dim(grad_values, key_start, WINDOW, 0) + value_part
        grad_values = lax.dynamic_update_slice_in_dim(grad_values, value_window, key_start, 0)
        return (grad_query, grad_keys, grad_values)

    zero_field = jnp.zeros(query.shape, WIDE_TYPE)
    return lax.fori_loop(0, row_count // BLOCK, one_block, (zero_field, zero_field, zero_field))


def local(
    patches,
    pos_embed,
    counts,
    ln1_gain,
    w_qkv,
    w_out,
    ln2_gain,
    w_up,
    w_down,
    ln3_gain,
    w_learn1,
    w_learn2,
    cotangent,
):
    row_count = patches.shape[0]
    width = patches.shape[1]
    head_width = w_qkv.shape[2]
    local_heads = head_width // HEAD_DIM
    score_scale = HEAD_DIM ** (-0.5)
    image_count = counts.shape[1]
    token_count = w_learn2.shape[1]
    inputs = patches.astype(WIDE_TYPE) + pos_embed.astype(WIDE_TYPE)
    image_of = image_ids(counts[0], row_count)
    member = (image_of[:, None] == jnp.arange(image_count, dtype=jnp.int32)[None, :]).astype(
        WIDE_TYPE
    )
    row_scale = jnp.sum(member * lax.rsqrt(counts[0].astype(WIDE_TYPE))[None, :], axis=1)
    norm_one, normed_one, inverse_one = layer_norm(inputs, ln1_gain)
    low_one = norm_one.astype(LOW_TYPE)
    qkv = jnp.einsum("td,dch->tch", low_one, w_qkv, preferred_element_type=WIDE_TYPE).astype(
        LOW_TYPE
    )
    query = qkv[:, 0].reshape(row_count, local_heads, HEAD_DIM)
    keys = qkv[:, 1].reshape(row_count, local_heads, HEAD_DIM)
    values = qkv[:, 2].reshape(row_count, local_heads, HEAD_DIM)
    mixed, log_sums = attend_forward(query, keys, values, image_of, score_scale)
    mixed_flat = mixed.reshape(row_count, head_width)
    attended = lax.psum(
        jnp.dot(mixed_flat, w_out, preferred_element_type=WIDE_TYPE).astype(jnp.bfloat16), "tensor"
    ).astype(jnp.float32)
    hidden = inputs + attended
    norm_two, normed_two, inverse_two = layer_norm(hidden, ln2_gain)
    low_two = norm_two.astype(LOW_TYPE)
    upper = jnp.dot(low_two, w_up, preferred_element_type=WIDE_TYPE)
    active = gelu_exact(upper).astype(LOW_TYPE)
    fed = lax.psum(
        jnp.dot(active, w_down, preferred_element_type=WIDE_TYPE).astype(jnp.bfloat16), "tensor"
    ).astype(jnp.float32)
    output = hidden + fed
    norm_three, normed_three, inverse_three = layer_norm(output, ln3_gain)
    low_three = norm_three.astype(LOW_TYPE)
    inner = jnp.dot(low_three, w_learn1, preferred_element_type=WIDE_TYPE)
    acted = gelu_exact(inner).astype(LOW_TYPE)
    logits = jnp.dot(acted, w_learn2, preferred_element_type=WIDE_TYPE)
    select = jax.nn.sigmoid(logits)
    weights = (select * row_scale[:, None]).astype(LOW_TYPE)
    table = (member.astype(LOW_TYPE)[:, :, None] * weights[:, None, :]).reshape(
        row_count, image_count * token_count
    )
    low_out = output.astype(LOW_TYPE)
    pooled = jnp.einsum("tj,td->jd", table, low_out, preferred_element_type=WIDE_TYPE)
    learned = pooled.reshape(image_count, token_count, width).astype(LOW_TYPE)
    grad_pooled = cotangent.reshape(image_count * token_count, width)
    grad_output = jnp.einsum("tj,jd->td", table, grad_pooled, preferred_element_type=WIDE_TYPE)
    grad_table = jnp.einsum("td,jd->tj", low_out, grad_pooled, preferred_element_type=WIDE_TYPE)
    grad_weights = jnp.sum(
        grad_table.reshape(row_count, image_count, token_count) * member[:, :, None], axis=1
    )
    grad_logits = (grad_weights * row_scale[:, None] * select * (1.0 - select)).astype(LOW_TYPE)
    grad_learn2 = jnp.einsum("tl,tk->lk", acted, grad_logits, preferred_element_type=WIDE_TYPE)
    grad_acted = jnp.einsum("tk,lk->tl", grad_logits, w_learn2, preferred_element_type=WIDE_TYPE)
    grad_inner = gelu_grad(inner, grad_acted).astype(LOW_TYPE)
    grad_learn1 = jnp.einsum("td,tl->dl", low_three, grad_inner, preferred_element_type=WIDE_TYPE)
    grad_norm3 = jnp.einsum("tl,dl->td", grad_inner, w_learn1, preferred_element_type=WIDE_TYPE)
    grad_from_three, grad_gain3 = norm_back(grad_norm3, ln3_gain, normed_three, inverse_three)
    grad_output = grad_output + grad_from_three
    grad_fed = grad_output.astype(LOW_TYPE)
    grad_down = jnp.einsum("tf,td->fd", active, grad_fed, preferred_element_type=WIDE_TYPE)
    grad_active = jnp.einsum("td,fd->tf", grad_fed, w_down, preferred_element_type=WIDE_TYPE)
    grad_upper = gelu_grad(upper, grad_active).astype(LOW_TYPE)
    grad_up = jnp.einsum("td,tf->df", low_two, grad_upper, preferred_element_type=WIDE_TYPE)
    grad_norm2 = lax.psum(
        jnp.einsum("tf,df->td", grad_upper, w_up, preferred_element_type=WIDE_TYPE).astype(
            jnp.bfloat16
        ),
        "tensor",
    ).astype(jnp.float32)
    grad_from_two, grad_gain2 = norm_back(grad_norm2, ln2_gain, normed_two, inverse_two)
    grad_hidden = grad_output + grad_from_two
    grad_attended = grad_hidden.astype(LOW_TYPE)
    grad_out_weight = jnp.einsum(
        "th,td->hd", mixed_flat, grad_attended, preferred_element_type=WIDE_TYPE
    )
    grad_mixed = jnp.einsum(
        "td,hd->th", grad_attended, w_out, preferred_element_type=WIDE_TYPE
    ).astype(LOW_TYPE)
    grad_mixed = grad_mixed.reshape(row_count, local_heads, HEAD_DIM)
    grad_query, grad_keys, grad_values = attend_backward(
        query, keys, values, image_of, log_sums, grad_mixed, score_scale
    )
    grad_qkv = (
        jnp.stack([grad_query, grad_keys, grad_values], axis=1)
        .reshape(row_count, 3, head_width)
        .astype(LOW_TYPE)
    )
    grad_qkv_weight = jnp.einsum("td,tch->dch", low_one, grad_qkv, preferred_element_type=WIDE_TYPE)
    grad_norm1 = lax.psum(
        jnp.einsum("tch,dch->td", grad_qkv, w_qkv, preferred_element_type=WIDE_TYPE).astype(
            jnp.bfloat16
        ),
        "tensor",
    ).astype(jnp.float32)
    grad_from_one, grad_gain1 = norm_back(grad_norm1, ln1_gain, normed_one, inverse_one)
    input_grad = (grad_hidden + grad_from_one).astype(LOW_TYPE)
    summed = (
        lax.psum(grad_gain1.astype(jnp.bfloat16), "dp").astype(jnp.float32),
        lax.psum(grad_qkv_weight.astype(jnp.bfloat16), "dp").astype(jnp.float32),
        lax.psum(grad_out_weight.astype(jnp.bfloat16), "dp").astype(jnp.float32),
        lax.psum(grad_gain2.astype(jnp.bfloat16), "dp").astype(jnp.float32),
        lax.psum(grad_up.astype(jnp.bfloat16), "dp").astype(jnp.float32),
        lax.psum(grad_down.astype(jnp.bfloat16), "dp").astype(jnp.float32),
        lax.psum(grad_gain3.astype(jnp.bfloat16), "dp").astype(jnp.float32),
        lax.psum(grad_learn1.astype(jnp.bfloat16), "dp").astype(jnp.float32),
        lax.psum(grad_learn2.astype(jnp.bfloat16), "dp").astype(jnp.float32),
    )
    return (
        learned,
        input_grad,
        summed[0],
        summed[1],
        summed[2],
        summed[3],
        summed[4],
        summed[5],
        summed[6],
        summed[7],
        summed[8],
    )


def solution(mesh):
    return jax.shard_map(
        local,
        mesh=mesh,
        in_specs=(
            P("dp", None),
            P("dp", None),
            P("dp", None),
            P(),
            P(None, None, "tensor"),
            P("tensor", None),
            P(),
            P(None, "tensor"),
            P("tensor", None),
            P(),
            P(),
            P(),
            P("dp", None, None),
        ),
        out_specs=(
            P("dp", None, None),
            P("dp", None),
            P(),
            P(None, None, "tensor"),
            P("tensor", None),
            P(),
            P(None, "tensor"),
            P("tensor", None),
            P(),
            P(),
            P(),
        ),
        check_vma=False,
    )
```

profile of v0, /device:TPU:0, one launch (start us, length us, event | category | flops | bytes accessed | tf_op | source)
XLA Modules:
  0.0 1307.9 jit_solution(3772105733460153413)
XLA Ops:
  21.8 62.9 %while.33 = (s32[]{:T(128)}, bf16[4,512,4,64]{1,3,2,0:T(8,128)(2,1)}, f32[4,4,512,1]{2,1,3,0:T(4,128)}, s32[4]{0:T(128)S(1)}, bf16[2048,4,64]{0,2,1:T(8,128)(2,1...) while((s32[]{:T(128)}, ...), condition=%wide.region_7.8_spmd, body=%wide.region_4.0_spmd.sunk | while | flops 914290688 | bytes 50817812 | solution.py:81
  92.9 157.8 %all-reduce.8.cloned.1.call-done = bf16[2048,1024]{1,0:T(8,128)(2,1)} async-done(((bf16[2048,1024]{1,0:T(8,128)(2,1)}), bf16[2048,1024]{1,0:T(8,128)(2,1)}) %all-reduce.8.cloned.1.call-update) | async-done | bytes 4194320 | tf_op jit(solution)/shard_map/psum | solution.py:159
  250.7 6.4 fusion.122
  261.4 24.0 %multiply_convert_fusion.3 = (bf16[2048,1024]{1,0:T(8,128)(2,1)S(1)}, f32[2048,1024]{1,0:T(8,128)}, f32[2048,1024]{1,0:T(8,128)}) fusion(bf16[2048,1024]{1,0:T(8,128)(2,1)S(1)} %multiply_convert_fusion.4, bf16[1024,1024]{1,0:T(8,128)(2,1)S(1)} %copy-done.55), kind=kOutput, calls=%fused_computation.98 | convolution fusion | flops 4431282176 | bytes 27262976 | tf_op jit(solution)/shard_map/dot_general | solution.py:165
  287.5 6.0 convolution_convert_fusion.2
  293.7 153.9 %all-reduce.10.cloned.1.call-done = bf16[2048,1024]{1,0:T(8,128)(2,1)} async-done(((bf16[2048,1024]{1,0:T(8,128)(2,1)}), bf16[2048,1024]{1,0:T(8,128)(2,1)}) %all-reduce.10.cloned.1.call-update) | async-done | bytes 4194320 | tf_op jit(solution)/shard_map/psum | solution.py:167
  455.9 22.9 %multiply_convert_fusion.1 = (bf16[2048,1024]{1,0:T(8,128)(2,1)S(1)}, f32[2048,1024]{1,0:T(8,128)S(1)}, f32[2048,1024]{1,0:T(8,128)}) fusion(bf16[2048,1024]{1,0:T(8,128)(2,1)S(1)} %multiply_convert_fusion.2, bf16[1024,1024]{1,0:T(8,128)(2,1)S(1)} %copy-done), kind=kOutput, calls=%fused_computation.82 | convolution fusion | flops 4431282176 | bytes 27262976 | tf_op jit(solution)/shard_map/dot_general | solution.py:173
  481.5 6.2 add_convert_fusion.1
  487.8 6.8 multiply_reduce_fusion.1
  500.0 13.5 %add_convert_fusion = bf16[2048,1024]{1,0:T(8,128)(2,1)S(1)} fusion(f32[2048,1024]{1,0:T(8,128)} %get-tuple-element.421, f32[2048,1024]{1,0:T(8,128)} %get-tuple-element.435, bf16[1024,1024]{1,0:T(8,128)(2,1)S(1)} %copy-done.54, f32[2048,1024]{1,0:T(8,128)} %bitcast_add_fusion), kind=kOutput, calls=%fused_computation.79 | convolution fusion | flops 4326424576 | bytes 31457280 | tf_op jit(solution)/shard_map/td,fd->tf/dot_general | solution.py:200
  515.5 6.3 convolution_convert_fusion.1
  523.0 9.7 convolution_convert_fusion.5
  532.8 6.2 convolution_convert_fusion.6
  544.8 131.2 %all-reduce.12.cloned.1.call-done = bf16[2048,1024]{1,0:T(8,128)(2,1)} async-done(((bf16[2048,1024]{1,0:T(8,128)(2,1)}), bf16[2048,1024]{1,0:T(8,128)(2,1)}) %all-reduce.12.cloned.1.call-update) | async-done | bytes 4194320 | tf_op jit(solution)/shard_map/psum | solution.py:203
  676.0 7.0 fusion.54
  683.0 7.7 fusion.52
  699.5 255.3 %while.34 = (s32[]{:T(128)}, bf16[2048,4,64]{0,2,1:T(8,128)(2,1)}, f32[2048,4,64]{0,2,1:T(8,128)}, f32[2048,4,64]{0,2,1:T(8,128)}, bf16[2048,4,64]{0,2,1:T(8,128...) while((s32[]{:T(128)}, bf16[2048,4,64]{0,2,1:T(8,128)(2,1)}, ...), condition=%wide.region_23.24_spmd, body=%wide.region_21.23_spmd.sunk | while | flops 2234415104 | bytes 213665648 | solution.py:118
  704.1 9.5 multiply_reduce_fusion.8
  713.6 7.3 multiply_convert_fusion.9
  727.2 10.2 dynamic_update_slice.55
  737.4 5.8 fusion.185
  743.2 10.4 fusion.187
  753.6 10.2 dynamic_update_slice.56
  768.2 9.5 multiply_reduce_fusion.8
  777.7 7.3 multiply_convert_fusion.9
  791.3 10.2 dynamic_update_slice.55
  801.5 5.8 fusion.185
  807.3 10.4 fusion.187
  817.7 10.2 dynamic_update_slice.56
  832.3 9.5 multiply_reduce_fusion.8
  841.8 7.3 multiply_convert_fusion.9
  855.4 9.8 dynamic_update_slice.55
  865.2 5.8 fusion.185
  871.1 10.4 fusion.187
  881.4 9.8 dynamic_update_slice.56
  895.7 9.5 multiply_reduce_fusion.8
  905.2 7.3 multiply_convert_fusion.9
  918.8 9.8 dynamic_update_slice.55
  928.6 5.8 fusion.185
  934.4 10.4 fusion.187
  944.8 9.8 dynamic_update_slice.56
  961.7 9.2 convolution_convert_fusion.7
  972.5 6.4 bitcast_convert_fusion
  986.9 111.4 %all-reduce.16.cloned.1.call-done = (bf16[1024,3,256]{2,0,1:T(8,128)(2,1)}, bf16[256,1024]{1,0:T(8,128)(2,1)}, bf16[1024,1024]{1,0:T(8,128)(2,1)}, bf16[1024,1024]{1,0:T(8,128)(2,1)}, bf16[1024,1024]{1,0:T(8,128)(2,1)}) async-done(((bf16[1024,3,256]{2,0,1:T(8,128)(2,1)}, bf16[256,1024]{1,0:T(8,128)(2,1)}, bf16[1024,1024]{1,0:T(8,128)(2,1)}, bf16[1024,1024]{1,0:T(8,128)(2,1)}, bf16[1024,1024]{1,0:T(8,128)(2,1)}), ...) | async-done | bytes 8388624 | tf_op jit(solution)/shard_map/psum | solution.py:238
  1112.2 144.2 %all-reduce.14.cloned.1.call-done = bf16[2048,1024]{1,0:T(8,128)(2,1)} async-done(((bf16[2048,1024]{1,0:T(8,128)(2,1)}), bf16[2048,1024]{1,0:T(8,128)(2,1)}) %all-reduce.14.cloned.1.call-update) | async-done | bytes 4194320 | tf_op jit(solution)/shard_map/psum | solution.py:228
  1256.4 7.0 fusion.60
  1263.4 24.0 %all-reduce = (bf16[1024]{0:T(1024)(128)(2,1)S(1)}, bf16[1024]{0:T(1024)(128)(2,1)S(1)}, bf16[1024]{0:T(1024)(128)(2,1)S(1)}, bf16[1024,8]{0,1:T(8,128)(2,1)S(1)}) all-reduce(bf16[1024]{0:T(1024)(128)(2,1)S(1)} %get-tuple-element.366, bf16[1024]{0:T(1024)(128)(2,1)S(1)} %copy-done.50, ...), channel_id=1, replica_groups=mesh['dp'=8,'tensor'=4] {'dp'}, use_global_device_ids=true, to_apply=%region_28.29 | all-reduce | flops 11264 | bytes 45056 | tf_op jit(solution)/shard_map/psum | solution.py:237
  1289.9 11.2 fusion.58
  (283 shorter events, 198.3 us)
Async XLA Ops:
  7.2 448.7 %copy-start = (bf16[1024,1024]{1,0:T(8,128)(2,1)S(1)}, bf16[1024,1024]{1,0:T(8,128)(2,1)}, u32[]{:S(2)}) copy-start(bf16[1024,1024]{1,0:T(8,128)(2,1)} %param.27) | copy-start | bytes 6291460
  7.2 243.5 %all-reduce.8.cloned.1.call-start = ((), (), s32[]{:S(2)}) async-start(), calls=%async_computation | async-start | bytes 8388608 | tf_op jit(solution)/shard_map/psum | solution.py:159
  7.3 7.8 copy-start.48
  7.3 7.8 copy-start.57
  13.3 6.5 copy-start.39
  15.2 6.4 copy-start.59
  84.8 8.1 copy-start.9
  84.8 208.9 %copy-start.24 = (s32[2048]{0:T(1024)}, s32[2048]{0:T(1024)S(1)}, u32[]{:S(2)}) copy-start(s32[2048]{0:T(1024)S(1)} %get-tuple-element.686) | copy-start | bytes 24580
  92.9 354.8 %all-reduce.10.cloned.1.call-start = ((), (), s32[]{:S(2)}) async-start(), calls=%async_computation.1 | async-start | bytes 8388608 | tf_op jit(solution)/shard_map/psum | solution.py:167
  258.2 27.1 %copy-start.41 = (f32[2048]{0:T(1024)}, f32[2048]{0:T(1024)S(1)}, u32[]{:S(2)}) copy-start(f32[2048]{0:T(1024)S(1)} %add_rsqrt_fusion.1) | copy-start | bytes 24580
  261.4 24.0 %copy-start.18 = (bf16[2048,1024]{1,0:T(8,128)(2,1)}, bf16[2048,1024]{1,0:T(8,128)(2,1)S(1)}, u32[]{:S(2)}) copy-start(bf16[2048,1024]{1,0:T(8,128)(2,1)S(1)} %multiply_convert_fusion.4) | copy-start | bytes 12582916
  261.4 26.1 %copy-start.53 = (bf16[1024,1024]{1,0:T(8,128)(2,1)S(1)}, bf16[1024,1024]{1,0:T(8,128)(2,1)}, u32[]{:S(2)}) copy-start(bf16[1024,1024]{1,0:T(8,128)(2,1)} %param.25) | copy-start | bytes 6291460
  293.5 382.5 %all-reduce.12.cloned.1.call-start = ((), (), s32[]{:S(2)}) async-start(), calls=%async_computation.2 | async-start | bytes 8388608 | tf_op jit(solution)/shard_map/psum | solution.py:203
  293.7 200.8 %copy-start.37 = (bf16[2048,8]{0,1:T(8,128)(2,1)}, bf16[2048,8]{0,1:T(8,128)(2,1)S(1)}, u32[]{:S(2)}) copy-start(bf16[2048,8]{0,1:T(8,128)(2,1)S(1)} %get-tuple-element.434) | copy-start | bytes 98308
  453.1 41.4 %copy-start.6 = (f32[2048,1024]{1,0:T(8,128)}, f32[2048,1024]{1,0:T(8,128)S(1)}, u32[]{:S(2)}) copy-start(f32[2048,1024]{1,0:T(8,128)S(1)} %get-tuple-element.419) | copy-start | bytes 25165828
  455.9 23.0 %copy-start.20 = (bf16[2048,1024]{1,0:T(8,128)(2,1)}, bf16[2048,1024]{1,0:T(8,128)(2,1)S(1)}, u32[]{:S(2)}) copy-start(bf16[2048,1024]{1,0:T(8,128)(2,1)S(1)} %multiply_convert_fusion.2) | copy-start | bytes 12582916
  455.9 22.9 %copy-start.58 = (bf16[8,8,1024]{2,1,0:T(8,128)(2,1)S(1)}, bf16[8,8,1024]{2,1,0:T(8,128)(2,1)}, u32[]{:S(2)}) copy-start(bf16[8,8,1024]{2,1,0:T(8,128)(2,1)} %param.29) | copy-start | bytes 393220
  481.5 13.0 copy-start.33
  487.7 6.8 copy-start.61
  500.0 15.6 %copy-start.56 = (bf16[1024,1024]{1,0:T(8,128)(2,1)S(1)}, bf16[1024,1024]{1,0:T(8,128)(2,1)}, u32[]{:S(2)}) copy-start(bf16[1024,1024]{1,0:T(8,128)(2,1)} %param.24) | copy-start | bytes 6291460
  521.9 576.4 %all-reduce.16.cloned.1.call-start = ((), (), s32[]{:S(2)}) async-start(), calls=%async_computation.4 | async-start | bytes 16777216 | tf_op jit(solution)/shard_map/psum | solution.py:238
  523.0 9.8 copy-start.19
  523.0 9.8 copy-start.63
  523.0 15.9 %slice-start = ((s8[8388608]{0:T(1024)(128)(4,1)}), s8[4194304]{0:T(1024)(128)(4,1)S(1)}, s32[]{:S(2)}) async-start(s8[8388608]{0:T(1024)(128)(4,1)} %bitcast.122), calls=%async_computation.5 | async-start | bytes 8388608
  539.0 137.1 %copy-start.32 = (f32[2048]{0:T(1024)S(1)}, f32[2048]{0:T(1024)}, u32[]{:S(2)}) copy-start(f32[2048]{0:T(1024)} %copy-done.31) | copy-start | bytes 24580
  539.0 137.1 %copy-start.42 = (f32[2048]{0:T(1024)S(1)}, f32[2048]{0:T(1024)}, u32[]{:S(2)}) copy-start(f32[2048]{0:T(1024)} %copy-done.41) | copy-start | bytes 24580
  539.0 137.0 %copy-start.46 = (f32[1024]{0:T(1024)S(1)}, f32[1024]{0:T(1024)}, u32[]{:S(2)}) copy-start(f32[1024]{0:T(1024)} %param.23) | copy-start | bytes 12292
  676.0 7.0 copy-start.15
  683.0 7.7 copy-start.23
  702.7 10.9 copy-start.2
  713.6 10.1 copy-start.11
  766.8 10.9 copy-start.2
  777.7 10.1 copy-start.11
  830.9 10.9 copy-start.2
  841.8 10.1 copy-start.11
  894.2 11.0 copy-start.2
  905.2 10.1 copy-start.11
  954.8 6.9 copy-start.40
  954.8 6.9 copy-start.44
  954.8 6.9 copy-start.49
  971.0 7.9 copy-start.36
  971.0 285.4 %all-reduce.14.cloned.1.call-start = ((), (), s32[]{:S(2)}) async-start(), calls=%async_computation.3 | async-start | bytes 8388608 | tf_op jit(solution)/shard_map/psum | solution.py:228
  1098.3 8.4 copy-start.22
  1098.3 10.8 copy-start.26
  1102.5 8.6 copy-start.30
  1109.2 154.2 %copy-start.50 = (bf16[1024]{0:T(1024)(128)(2,1)S(1)}, bf16[1024]{0:T(1024)(128)(2,1)}, u32[]{:S(2)}) copy-start(bf16[1024]{0:T(1024)(128)(2,1)} %get-tuple-element.364) | copy-start | bytes 6148
  1109.2 154.2 %copy-start.52 = (bf16[1024]{0:T(1024)(128)(2,1)S(1)}, bf16[1024]{0:T(1024)(128)(2,1)}, u32[]{:S(2)}) copy-start(bf16[1024]{0:T(1024)(128)(2,1)} %get-tuple-element.362) | copy-start | bytes 6148
  1289.8 11.2 copy-start.1
  (37 other events, 133.6 us)
Sparse Core Ops, SparseCore 0:
  93.0 157.6 all-reduce.7
  293.6 153.9 all-reduce.9
  522.0 153.9 all-reduce.11
  971.1 127.1 all-reduce.15
  1101.1 155.2 all-reduce.13
where the time goes:
time: 1320 us; the launch traced here: 1310 us
  waiting for transfers between devices  699 us (53%)
  matrix products  319 us (24%)
  other arithmetic  128 us (10%)
  local copies, waits for them, and re-layouts  119 us (9%)
  blocking collectives  24 us (2%)
  between operations  14.9 us (1%)
    psum x1, waiting for transfers between devices, local(): lax.psum(jnp.dot(mixed_flat, w_out, preferred_element_type=WIDE_TYPE).ast...  158 us
    psum x1, waiting for transfers between devices, local(): lax.psum(jnp.dot(active, w_down, preferred_element_type=WIDE_TYPE).astype...  154 us
    psum x1, waiting for transfers between devices, local(): lax.psum(jnp.einsum('tch,dch->td', grad_qkv, w_qkv, preferred_element_typ...  144 us
    psum x1, waiting for transfers between devices, local(): lax.psum(jnp.einsum('tf,df->td', grad_upper, w_up, preferred_element_type...  131 us
    psum x1, waiting for transfers between devices, local(): lax.psum(grad_qkv_weight.astype(jnp.bfloat16), 'dp').astype(jnp.float32)  111 us
    dot_general x4, matrix products, one_block(): jnp.einsum('hqk,qhd->khd', probs.astype(LOW_TYPE), grad_block, preferred_...  41.5 us
    dynamic_update_slice x4, local copies, waits for them, and re-layouts, one_block(): lax.dynamic_update_slice_in_dim(grad_values, value_window, key_start, 0)  40 us
    dynamic_update_slice x4, local copies, waits for them, and re-layouts, one_block(): lax.dynamic_update_slice_in_dim(grad_keys, key_window, key_start, 0)  40 us
  transfers between devices with their start and end apart: 5, of which 5 were waited for; matrix products, arithmetic and copies ran while one was open for 4% of the time, Pallas kernels for 0%

commit v1 on v0

--- a/solution.py
+++ b/solution.py
@@ -235,7 +235,9 @@
     input_grad = (grad_hidden + grad_from_one).astype(LOW_TYPE)
     summed = (
         lax.psum(grad_gain1.astype(jnp.bfloat16), "dp").astype(jnp.float32),
-        lax.psum(grad_qkv_weight.astype(jnp.bfloat16), "dp").astype(jnp.float32),
+        jnp.sum(lax.all_gather(grad_qkv_weight.astype(jnp.bfloat16), "dp"), axis=0).astype(
+            jnp.float32
+        ),
         lax.psum(grad_out_weight.astype(jnp.bfloat16), "dp").astype(jnp.float32),
         lax.psum(grad_gain2.astype(jnp.bfloat16), "dp").astype(jnp.float32),
         lax.psum(grad_up.astype(jnp.bfloat16), "dp").astype(jnp.float32),

time: 1320 us -> 1240 us (0.939)
  waiting for transfers between devices: 699 us -> 596 us
    psum x1, waiting for transfers between devices: 111 us -> 0.01 us  [local(): lax.psum(grad_out_weight.astype(jnp.bfloat16), 'dp').astype(jnp.float32)]
    all_gather x0 -> x1, waiting for transfers between devices: none -> 27.2 us  [local(): lax.all_gather(grad_qkv_weight.astype(jnp.bfloat16), 'dp')]
    psum x1, waiting for transfers between devices: 144 us -> 126 us  [local(): lax.psum(jnp.einsum('tch,dch->td', grad_qkv, w_qkv, preferred_element_typ...]
  transfers between devices with their start and end apart: 5 -> 6, of which waited for: 5 -> 5; matrix products, arithmetic and copies ran while one was open for 4% -> 27% of each run, Pallas kernels for 0% -> 0%
where the time goes in v1:
time: 1240 us; the launch traced here: 1220 us
  waiting for transfers between devices  596 us (48%)
  matrix products  324 us (26%)
  other arithmetic  139 us (11%)
  local copies, waits for them, and re-layouts  120 us (10%)
  blocking collectives  24.7 us (2%)
  between operations  15.3 us (1%)
    psum x1, waiting for transfers between devices, local(): lax.psum(jnp.dot(mixed_flat, w_out, preferred_element_type=WIDE_TYPE).ast...  158 us
    psum x1, waiting for transfers between devices, local(): lax.psum(jnp.dot(active, w_down, preferred_element_type=WIDE_TYPE).astype...  154 us
    psum x1, waiting for transfers between devices, local(): lax.psum(jnp.einsum('tf,df->td', grad_upper, w_up, preferred_element_type...  131 us
    psum x1, waiting for transfers between devices, local(): lax.psum(jnp.einsum('tch,dch->td', grad_qkv, w_qkv, preferred_element_typ...  126 us
    dot_general x4, matrix products, one_block(): jnp.einsum('hqk,qhd->khd', probs.astype(LOW_TYPE), grad_block, preferred_...  41.7 us
    dynamic_update_slice x4, local copies, waits for them, and re-layouts, one_block(): lax.dynamic_update_slice_in_dim(grad_values, value_window, key_start, 0)  40.2 us
    dynamic_update_slice x4, local copies, waits for them, and re-layouts, one_block(): lax.dynamic_update_slice_in_dim(grad_keys, key_window, key_start, 0)  40.1 us
    dot_general x4, matrix products, one_block(): jnp.einsum('qhd,khd->hqk', grad_block, value_block, preferred_element_typ...  38.3 us
  transfers between devices with their start and end apart: 6, of which 5 were waited for; matrix products, arithmetic and copies ran while one was open for 27% of the time, Pallas kernels for 0%

profile of v1, /device:TPU:0, one launch (start us, length us, event | category | flops | bytes accessed | tf_op | source)
XLA Modules:
  0.0 1223.3 jit_solution(713076502923570012)
XLA Ops:
  21.8 62.9 %while.33 = (s32[]{:T(128)}, bf16[4,512,4,64]{1,3,2,0:T(8,128)(2,1)}, f32[4,4,512,1]{2,1,3,0:T(4,128)}, s32[4]{0:T(128)S(1)}, bf16[2048,4,64]{0,2,1:T(8,128)(2,1...) while((s32[]{:T(128)}, ...), condition=%wide.region_7.8_spmd, body=%wide.region_4.0_spmd.sunk | while | flops 914290688 | bytes 50817812 | solution.py:81
  92.9 157.8 %all-reduce.8.cloned.1.call-done = bf16[2048,1024]{1,0:T(8,128)(2,1)} async-done(((bf16[2048,1024]{1,0:T(8,128)(2,1)}), bf16[2048,1024]{1,0:T(8,128)(2,1)}) %all-reduce.8.cloned.1.call-update) | async-done | bytes 4194320 | tf_op jit(solution)/shard_map/psum | solution.py:159
  250.7 6.4 fusion.122
  261.4 24.0 %multiply_convert_fusion.3 = (bf16[2048,1024]{1,0:T(8,128)(2,1)S(1)}, f32[2048,1024]{1,0:T(8,128)}, f32[2048,1024]{1,0:T(8,128)}) fusion(bf16[2048,1024]{1,0:T(8,128)(2,1)S(1)} %multiply_convert_fusion.4, bf16[1024,1024]{1,0:T(8,128)(2,1)S(1)} %copy-done.53), kind=kOutput, calls=%fused_computation.98 | convolution fusion | flops 4431282176 | bytes 27262976 | tf_op jit(solution)/shard_map/dot_general | solution.py:165
  287.5 6.0 convolution_convert_fusion.2
  293.7 153.9 %all-reduce.10.cloned.1.call-done = bf16[2048,1024]{1,0:T(8,128)(2,1)} async-done(((bf16[2048,1024]{1,0:T(8,128)(2,1)}), bf16[2048,1024]{1,0:T(8,128)(2,1)}) %all-reduce.10.cloned.1.call-update) | async-done | bytes 4194320 | tf_op jit(solution)/shard_map/psum | solution.py:167
  455.9 22.9 %multiply_convert_fusion.1 = (bf16[2048,1024]{1,0:T(8,128)(2,1)S(1)}, f32[2048,1024]{1,0:T(8,128)S(1)}, f32[2048,1024]{1,0:T(8,128)}) fusion(bf16[2048,1024]{1,0:T(8,128)(2,1)S(1)} %multiply_convert_fusion.2, bf16[1024,1024]{1,0:T(8,128)(2,1)S(1)} %copy-done), kind=kOutput, calls=%fused_computation.82 | convolution fusion | flops 4431282176 | bytes 27262976 | tf_op jit(solution)/shard_map/dot_general | solution.py:173
  481.5 6.2 add_convert_fusion.1
  487.7 6.8 multiply_reduce_fusion.1
  499.9 13.6 %add_convert_fusion = bf16[2048,1024]{1,0:T(8,128)(2,1)S(1)} fusion(f32[2048,1024]{1,0:T(8,128)} %get-tuple-element.420, f32[2048,1024]{1,0:T(8,128)} %get-tuple-element.434, bf16[1024,1024]{1,0:T(8,128)(2,1)S(1)} %copy-done.52, f32[2048,1024]{1,0:T(8,128)} %bitcast_add_fusion), kind=kOutput, calls=%fused_computation.79 | convolution fusion | flops 4326424576 | bytes 31457280 | tf_op jit(solution)/shard_map/td,fd->tf/dot_general | solution.py:200
  515.5 6.3 convolution_convert_fusion.1
  523.0 9.7 convolution_convert_fusion.5
  532.8 6.2 convolution_convert_fusion.6
  544.8 131.3 %all-reduce.12.cloned.1.call-done = bf16[2048,1024]{1,0:T(8,128)(2,1)} async-done(((bf16[2048,1024]{1,0:T(8,128)(2,1)}), bf16[2048,1024]{1,0:T(8,128)(2,1)}) %all-reduce.12.cloned.1.call-update) | async-done | bytes 4194320 | tf_op jit(solution)/shard_map/psum | solution.py:203
  676.0 7.0 fusion.54
  683.0 7.7 fusion.52
  705.0 256.6 %while.34 = (s32[]{:T(128)}, bf16[2048,4,64]{0,2,1:T(8,128)(2,1)}, f32[2048,4,64]{0,2,1:T(8,128)}, f32[2048,4,64]{0,2,1:T(8,128)}, bf16[2048,4,64]{0,2,1:T(8,128...) while((s32[]{:T(128)}, bf16[2048,4,64]{0,2,1:T(8,128)(2,1)}, ...), condition=%wide.region_23.24_spmd, body=%wide.region_21.23_spmd.sunk | while | flops 2234415104 | bytes 213665648 | solution.py:118
  709.6 9.5 multiply_reduce_fusion.8
  719.1 7.6 multiply_convert_fusion.9
  732.9 10.3 dynamic_update_slice.55
  743.2 5.9 fusion.185
  749.0 10.6 fusion.187
  759.6 10.4 dynamic_update_slice.56
  774.4 9.9 multiply_reduce_fusion.8
  784.2 7.6 multiply_convert_fusion.9
  798.0 10.3 dynamic_update_slice.55
  814.1 10.4 fusion.187
  824.5 10.2 dynamic_update_slice.56
  839.2 9.5 multiply_reduce_fusion.8
  848.6 7.3 multiply_convert_fusion.9
  862.2 9.8 dynamic_update_slice.55
  872.0 5.8 fusion.185
  877.9 10.4 fusion.187
  888.3 9.8 dynamic_update_slice.56
  902.5 9.5 multiply_reduce_fusion.8
  912.0 7.3 multiply_convert_fusion.9
  925.6 9.8 dynamic_update_slice.55
  935.4 5.8 fusion.185
  941.2 10.4 fusion.187
  951.6 9.8 dynamic_update_slice.56
  968.3 7.7 bitcast_convert_fusion
  976.2 9.1 convolution_convert_fusion.7
  1004.9 125.9 %all-reduce.14.cloned.1.call-done = bf16[2048,1024]{1,0:T(8,128)(2,1)} async-done(((bf16[2048,1024]{1,0:T(8,128)(2,1)}), bf16[2048,1024]{1,0:T(8,128)(2,1)}) %all-reduce.14.cloned.1.call-update) | async-done | bytes 4194320 | tf_op jit(solution)/shard_map/psum | solution.py:228
  1130.7 7.2 fusion.60
  1138.0 24.7 %all-reduce = (bf16[1024]{0:T(1024)(128)(2,1)S(1)}, bf16[1024]{0:T(1024)(128)(2,1)S(1)}, bf16[1024]{0:T(1024)(128)(2,1)S(1)}, bf16[1024,8]{0,1:T(8,128)(2,1)S(1)}) all-reduce(bf16[1024]{0:T(1024)(128)(2,1)S(1)} %get-tuple-element.366, bf16[1024]{0:T(1024)(128)(2,1)S(1)} %copy-done.48, ...), channel_id=1, replica_groups=mesh['dp'=8,'tensor'=4] {'dp'}, use_global_device_ids=true, to_apply=%region_28.29 | all-reduce | flops 11264 | bytes 45056 | tf_op jit(solution)/shard_map/psum | solution.py:237
  1165.1 12.3 %fusion.58 = bf16[2048,1024]{1,0:T(8,128)(2,1)} fusion(f32[2048,1024]{1,0:T(8,128)} %copy-done.5, bf16[2048,1024]{1,0:T(8,128)(2,1)} %all-reduce.14.cloned.1.call-done, f32[2048]{0:T(1024)S(1)} %broadcast_multiply_fusion, f32[2048]{0:T(1024)S(1)} %broadcast_multiply_fusion.1, f32[1024]{0:T(1024)S(1)} %copy-done.47, f32[2048]{0:T(1024)S(1)} %copy-done.42, ...), kind=kLoop, calls=%fused_computation.71 | loop fusion | flops 27262976 | bytes 25202688 | tf_op jit(solution)/shard_map/convert_element_type | solution.py:235
  1177.4 27.2 %all-gather.3.cloned.1.call-done = bf16[8192,3,256]{2,0,1:T(8,128)(2,1)} async-done(((bf16[1024,3,256]{2,0,1:T(8,128)(2,1)}), bf16[8192,3,256]{2,0,1:T(8,128)(2,1)}) %all-gather.3.cloned.1.call-update) | async-done | bytes 12582928 | tf_op jit(solution)/shard_map/all_gather | solution.py:238
  1204.6 8.0 reduce_sum.218
  (283 shorter events, 209.2 us)
Async XLA Ops:
  7.2 448.7 %copy-start = (bf16[1024,1024]{1,0:T(8,128)(2,1)S(1)}, bf16[1024,1024]{1,0:T(8,128)(2,1)}, u32[]{:S(2)}) copy-start(bf16[1024,1024]{1,0:T(8,128)(2,1)} %param.27) | copy-start | bytes 6291460
  7.2 243.5 %all-reduce.8.cloned.1.call-start = ((), (), s32[]{:S(2)}) async-start(), calls=%async_computation | async-start | bytes 8388608 | tf_op jit(solution)/shard_map/psum | solution.py:159
  7.3 7.8 copy-start.46
  7.3 7.8 copy-start.55
  84.8 8.1 copy-start.9
  84.8 208.9 %copy-start.24 = (s32[2048]{0:T(1024)}, s32[2048]{0:T(1024)S(1)}, u32[]{:S(2)}) copy-start(s32[2048]{0:T(1024)S(1)} %get-tuple-element.685) | copy-start | bytes 24580
  92.9 354.8 %all-reduce.10.cloned.1.call-start = ((), (), s32[]{:S(2)}) async-start(), calls=%async_computation.1 | async-start | bytes 8388608 | tf_op jit(solution)/shard_map/psum | solution.py:167
  258.3 27.1 %copy-start.39 = (f32[2048]{0:T(1024)}, f32[2048]{0:T(1024)S(1)}, u32[]{:S(2)}) copy-start(f32[2048]{0:T(1024)S(1)} %add_rsqrt_fusion.1) | copy-start | bytes 24580
  261.4 24.0 %copy-start.18 = (bf16[2048,1024]{1,0:T(8,128)(2,1)}, bf16[2048,1024]{1,0:T(8,128)(2,1)S(1)}, u32[]{:S(2)}) copy-start(bf16[2048,1024]{1,0:T(8,128)(2,1)S(1)} %multiply_convert_fusion.4) | copy-start | bytes 12582916
  261.4 26.1 %copy-start.51 = (bf16[1024,1024]{1,0:T(8,128)(2,1)S(1)}, bf16[1024,1024]{1,0:T(8,128)(2,1)}, u32[]{:S(2)}) copy-start(bf16[1024,1024]{1,0:T(8,128)(2,1)} %param.25) | copy-start | bytes 6291460
  293.5 382.5 %all-reduce.12.cloned.1.call-start = ((), (), s32[]{:S(2)}) async-start(), calls=%async_computation.2 | async-start | bytes 8388608 | tf_op jit(solution)/shard_map/psum | solution.py:203
  293.7 200.8 %copy-start.35 = (bf16[2048,8]{0,1:T(8,128)(2,1)}, bf16[2048,8]{0,1:T(8,128)(2,1)S(1)}, u32[]{:S(2)}) copy-start(bf16[2048,8]{0,1:T(8,128)(2,1)S(1)} %get-tuple-element.433) | copy-start | bytes 98308
  453.1 41.4 %copy-start.6 = (f32[2048,1024]{1,0:T(8,128)}, f32[2048,1024]{1,0:T(8,128)S(1)}, u32[]{:S(2)}) copy-start(f32[2048,1024]{1,0:T(8,128)S(1)} %get-tuple-element.418) | copy-start | bytes 25165828
  455.9 23.0 %copy-start.20 = (bf16[2048,1024]{1,0:T(8,128)(2,1)}, bf16[2048,1024]{1,0:T(8,128)(2,1)S(1)}, u32[]{:S(2)}) copy-start(bf16[2048,1024]{1,0:T(8,128)(2,1)S(1)} %multiply_convert_fusion.2) | copy-start | bytes 12582916
  455.9 23.0 %copy-start.56 = (bf16[8,8,1024]{2,1,0:T(8,128)(2,1)S(1)}, bf16[8,8,1024]{2,1,0:T(8,128)(2,1)}, u32[]{:S(2)}) copy-start(bf16[8,8,1024]{2,1,0:T(8,128)(2,1)} %param.29) | copy-start | bytes 393220
  481.5 13.0 %copy-start.31 = (bf16[2048,8]{0,1:T(8,128)(2,1)}, bf16[2048,8]{0,1:T(8,128)(2,1)S(1)}, u32[]{:S(2)}) copy-start(bf16[2048,8]{0,1:T(8,128)(2,1)S(1)} %get-tuple-element.431) | copy-start | bytes 98308
  499.9 15.6 %copy-start.54 = (bf16[1024,1024]{1,0:T(8,128)(2,1)S(1)}, bf16[1024,1024]{1,0:T(8,128)(2,1)}, u32[]{:S(2)}) copy-start(bf16[1024,1024]{1,0:T(8,128)(2,1)} %param.24) | copy-start | bytes 6291460
  521.9 471.1 %all-reduce.16.cloned.1.call-start = ((), (), s32[]{:S(2)}) async-start(), calls=%async_computation.5 | async-start | bytes 13631488 | tf_op jit(solution)/shard_map/psum | solution.py:241
  523.0 9.7 copy-start.19
  523.0 9.7 copy-start.61
  523.0 15.9 %slice-start = ((s8[8388608]{0:T(1024)(128)(4,1)}), s8[4194304]{0:T(1024)(128)(4,1)S(1)}, s32[]{:S(2)}) async-start(s8[8388608]{0:T(1024)(128)(4,1)} %bitcast.124), calls=%async_computation.6 | async-start | bytes 8388608
  538.9 137.1 %copy-start.30 = (f32[2048]{0:T(1024)S(1)}, f32[2048]{0:T(1024)}, u32[]{:S(2)}) copy-start(f32[2048]{0:T(1024)} %copy-done.29) | copy-start | bytes 24580
  538.9 137.1 %copy-start.40 = (f32[2048]{0:T(1024)S(1)}, f32[2048]{0:T(1024)}, u32[]{:S(2)}) copy-start(f32[2048]{0:T(1024)} %copy-done.39) | copy-start | bytes 24580
  539.0 137.1 %copy-start.44 = (f32[1024]{0:T(1024)S(1)}, f32[1024]{0:T(1024)}, u32[]{:S(2)}) copy-start(f32[1024]{0:T(1024)} %param.23) | copy-start | bytes 12292
  683.0 11.1 copy-start.17
  701.8 428.9 %all-reduce.14.cloned.1.call-start = ((), (), s32[]{:S(2)}) async-start(), calls=%async_computation.3 | async-start | bytes 8388608 | tf_op jit(solution)/shard_map/psum | solution.py:228
  708.2 10.9 copy-start.2
  719.1 10.3 copy-start.11
  772.9 11.3 copy-start.2
  784.2 10.3 copy-start.11
  837.7 10.9 copy-start.2
  848.6 10.1 copy-start.11
  901.0 10.9 copy-start.2
  912.0 10.1 copy-start.11
  968.3 7.8 copy-start.26
  968.3 7.8 copy-start.27
  968.3 7.8 copy-start.38
  968.3 7.8 copy-start.42
  968.3 7.8 copy-start.47
  976.0 9.2 copy-start.34
  976.0 12.1 copy-start.32
  976.1 12.0 copy-start.36
  976.1 228.5 %all-gather.3.cloned.1.call-start = ((), (), s32[]{:S(2)}) async-start(), calls=%async_computation.4 | async-start | bytes 14155776 | tf_op jit(solution)/shard_map/all_gather | solution.py:238
  993.0 8.3 copy-start.22
  993.0 10.8 copy-start.28
  1003.8 134.2 %copy-start.48 = (bf16[1024]{0:T(1024)(128)(2,1)S(1)}, bf16[1024]{0:T(1024)(128)(2,1)}, u32[]{:S(2)}) copy-start(bf16[1024]{0:T(1024)(128)(2,1)} %get-tuple-element.364) | copy-start | bytes 6148
  1003.8 134.2 %copy-start.50 = (bf16[1024]{0:T(1024)(128)(2,1)S(1)}, bf16[1024]{0:T(1024)(128)(2,1)}, u32[]{:S(2)}) copy-start(bf16[1024]{0:T(1024)(128)(2,1)} %get-tuple-element.362) | copy-start | bytes 6148
  1204.6 11.4 copy-start.1
  (36 other events, 143.0 us)
Sparse Core Ops, SparseCore 0:
  93.0 157.6 all-reduce.7
  293.6 153.9 all-reduce.9
  522.0 153.9 all-reduce.11
  701.9 109.6 all-reduce.15
  976.2 154.5 all-reduce.13
  1133.2 71.3 all-gather.2
